TPU v7x, 32 devices: a whole 2x2x4 slice. The times are simulated.
32 devices in a mesh: section: 2 (over y), batch: 16 (over z, x, core).
Axes of the slice: x: 2, y: 2, z: 4, core: 2. Of those that a mesh axis runs over, the one named last changes fastest.
Arguments:
- images: bfloat16 [32, 64, 3072], P('batch', None, 'section'), may hold values from -1 to 1
- noise_draw: bfloat16 [32, 64, 3072], P('batch', None, 'section'), may hold values from -6 to 6
- cotangent: bfloat16 [32, 64, 3072], P('batch', None, 'section'), may hold values from -6 to 6
- hue_angle: float32 [32], P('batch'), may hold values from -0.5 to 0.5
- saturation: float32 [32], P('batch'), may hold values from 0.5 to 1.5
- timestep: int32 [32], P('batch'), may hold values from 50 to 199
- stem_weight: bfloat16 [3072, 1024], P('section'), may hold values from -0.109375 to 0.109375
- conv_weight: bfloat16 [2, 9216, 1024], P('section', 'batch'), may hold values from -0.0625 to 0.0625
- emb_weight: bfloat16 [2, 1024, 2048], P('section'), may hold values from -0.1875 to 0.1875
- head_weight: bfloat16 [1024, 3072], P(None, 'section'), may hold values from -0.1875 to 0.1875
Outputs:
- purified: bfloat16 [32, 64, 3072], P('batch', None, 'section')
- colour_grad: float32 [32, 2], P('batch')
All inputs are finite; a program needn't handle non-finite values.
Results may differ from a plain program's by a relative error of at most 0.039.
Values may be sent and summed in bfloat16 or wider, within the bound.
A program may use at most 128 MiB of HBM per device.

v0:
```python
import math
import jax
import jax.numpy as jnp
from jax import lax
from jax.sharding import PartitionSpec as P

CH = 1024
GROUPS = 32
TEMB = 1024
GRID = 8
TSTEPS = 1000
PV = 3072


def shifted(value, axis, steps):
    count = lax.axis_size(axis)
    pairs = [(source, (source + steps) % count) for source in range(count)]
    return lax.ppermute(value, axis, pairs)


def from_root(block, axis, holder):
    block = jnp.where(lax.axis_index(axis) == holder, block, jnp.zeros_like(block))
    return lax.psum(block, axis)


def noise_levels(timestep):
    beta_rates = jnp.linspace(0.0001, 0.02, TSTEPS, dtype=jnp.float32)
    levels = jnp.cumprod(1.0 - beta_rates)
    chosen = jnp.arange(TSTEPS, dtype=jnp.int32)[None, :] == timestep[:, None]
    return jnp.sum(jnp.where(chosen, levels[None, :], jnp.float32(0.0)), axis=1)


def time_features(timestep):
    half_width = TEMB // 2
    frequency = jnp.exp(-math.log(10000.0) * jnp.arange(half_width, dtype=jnp.float32) / half_width)
    angles = timestep.astype(jnp.float32)[:, None] * frequency[None, :]
    return jax.nn.silu(jnp.concatenate([jnp.cos(angles), jnp.sin(angles)], axis=1)).astype(
        jnp.bfloat16
    )


def colour_maps(hue_angle, saturation):
    grey_map = jnp.full((3, 3), 1.0 / 3.0, dtype=jnp.float32)
    rotate_map = jnp.eye(3, dtype=jnp.float32) - grey_map
    cross_map = jnp.array(
        [[0.0, -1.0, 1.0], [1.0, 0.0, -1.0], [-1.0, 1.0, 0.0]], dtype=jnp.float32
    ) / math.sqrt(3.0)
    cosine = jnp.cos(hue_angle)[:, None, None]
    sine_of = jnp.sin(hue_angle)[:, None, None]
    turning = cosine * rotate_map + sine_of * cross_map
    sat_scale = saturation[:, None, None]
    matrix = grey_map + sat_scale * turning
    hue_slope = sat_scale * (cosine * cross_map - sine_of * rotate_map)
    return (matrix, hue_slope, turning)


def apply_map(matrix, pixels):
    return jnp.sum(matrix[:, None, None, :, :] * pixels[:, :, :, None, :], axis=-1)


def conv_branch(feature, weight, scaling):
    number = feature.shape[0]
    channels = feature.shape[2]
    grouped = feature.reshape(number, GRID * GRID, GROUPS, channels // GROUPS)
    centre = jnp.mean(grouped, axis=(1, 3), keepdims=True)
    spread_sq = jnp.mean(jnp.square(grouped - centre), axis=(1, 3), keepdims=True)
    normed = ((grouped - centre) * lax.rsqrt(spread_sq + 1e-05)).reshape(
        number, GRID * GRID, channels
    )
    factor = scaling[:, None, :channels]
    offset = scaling[:, None, channels:]
    active = jax.nn.silu(normed * (1.0 + factor) + offset).astype(jnp.bfloat16)
    padded = jnp.pad(active.reshape(number, GRID, GRID, channels), ((0, 0), (1, 1), (1, 1), (0, 0)))
    taps = [
        padded[:, row_tap : row_tap + GRID, col_tap : col_tap + GRID, :]
        for row_tap in range(3)
        for col_tap in range(3)
    ]
    columns = jnp.concatenate(taps, axis=-1).reshape(number * GRID * GRID, 9 * channels)
    product = jnp.dot(columns, weight, preferred_element_type=jnp.float32)
    return product.reshape(number, GRID * GRID, channels)


def residual_block(feature, weight, scaling):
    primal = feature.astype(jnp.float32)
    return (primal + conv_branch(primal, weight, scaling)).astype(jnp.bfloat16)


def block_adjoint(feature, weight, scaling, upstream):
    primal = feature.astype(jnp.float32)

    def branch_only(probe):
        return conv_branch(probe, weight, scaling)

    _, pullback = jax.vjp(branch_only, primal)
    upstream_f = upstream.astype(jnp.float32)
    return (upstream_f + pullback(upstream_f)[0]).astype(jnp.bfloat16)


def section_total(partial_sum):
    return lax.psum(partial_sum.astype(jnp.bfloat16), "section").astype(jnp.float32)


def send_forward(value):
    return shifted(value, "section", 1)


def send_backward(value):
    return shifted(value, "section", -1)


def spread(value, owner):
    return from_root(value, "section", owner)


def store_one(buffer, value, index_at, is_live):
    previous = lax.dynamic_index_in_dim(buffer, index_at, 0, keepdims=False)
    return lax.dynamic_update_index_in_dim(buffer, jnp.where(is_live, value, previous), index_at, 0)


def run_chain(position, entering, worker, sender):
    number = entering.shape[0]
    clocks = number + lax.axis_size("section") - 1

    def advance(clock, state_in):
        incoming, sources, results = state_in
        member = clock - position
        is_live = (member >= 0) & (member < number)
        index_at = jnp.clip(member, 0, number - 1)
        entry_row = lax.dynamic_index_in_dim(entering, index_at, 0, keepdims=False)
        source = jnp.where(position == 0, entry_row, incoming)

        def run_work():
            return worker(source, index_at)

        def pass_through():
            return source

        result = lax.cond(is_live, run_work, pass_through)
        sources = store_one(sources, source, index_at, is_live)
        results = store_one(results, result, index_at, is_live)
        return (sender(result), sources, results)

    start = (jnp.zeros_like(entering[0]), jnp.zeros_like(entering), jnp.zeros_like(entering))
    final_state = lax.fori_loop(0, clocks, advance, start)
    return (final_state[1], final_state[2])


def local(
    images,
    noise_draw,
    cotangent,
    hue_angle,
    saturation,
    timestep,
    stem_weight,
    conv_weight,
    emb_weight,
    head_weight,
):
    sections = lax.axis_size("section")
    place = lax.axis_index("section")
    number = images.shape[0]
    columns_here = images.shape[2]
    full_conv = lax.all_gather(conv_weight, "batch", axis=1, tiled=True)[0]
    level = noise_levels(timestep)
    root_level = jnp.sqrt(level)[:, None, None]
    root_noise = jnp.sqrt(1.0 - level)[:, None, None]
    matrix, hue_slope, sat_slope = colour_maps(hue_angle, saturation)
    pixels = images.astype(jnp.float32).reshape(number, GRID * GRID, columns_here // 3, 3)
    coloured = apply_map(matrix, pixels).reshape(number, GRID * GRID, columns_here)
    noised = root_level * coloured + root_noise * noise_draw.astype(jnp.float32)
    entry_part = jnp.dot(
        noised.astype(jnp.bfloat16).reshape(-1, columns_here),
        stem_weight,
        preferred_element_type=jnp.float32,
    )
    first = section_total(entry_part).astype(jnp.bfloat16).reshape(number, GRID * GRID, CH)
    offsets = jnp.dot(time_features(timestep), emb_weight[0], preferred_element_type=jnp.float32)

    def forward_work(source, index_at):
        scaling = lax.dynamic_slice_in_dim(offsets, index_at, 1, 0)
        return residual_block(source[None], full_conv, scaling)[0]

    fwd_inputs, fwd_outputs = run_chain(place, first, forward_work, send_forward)
    finals = spread(fwd_outputs, sections - 1)
    predicted = jnp.dot(finals.reshape(-1, CH), head_weight, preferred_element_type=jnp.float32)
    predicted = predicted.reshape(number, GRID * GRID, columns_here)
    purified = ((noised - root_noise * predicted) / root_level).astype(jnp.bfloat16)
    weighted = cotangent.astype(jnp.float32) * (1.0 / math.sqrt(GRID * GRID * PV))
    eps_grad = (-(root_noise / root_level) * weighted).astype(jnp.bfloat16)
    seed_part = lax.dot_general(
        eps_grad.reshape(-1, columns_here),
        head_weight,
        (((1,), (1,)), ((), ())),
        preferred_element_type=jnp.float32,
    )
    seed = section_total(seed_part).astype(jnp.bfloat16).reshape(number, GRID * GRID, CH)

    def adjoint_work(source, index_at):
        saved = lax.dynamic_index_in_dim(fwd_inputs, index_at, 0, keepdims=True)
        scaling = lax.dynamic_slice_in_dim(offsets, index_at, 1, 0)
        return block_adjoint(saved, full_conv, scaling, source[None])[0]

    back_inputs, back_outputs = run_chain(sections - 1 - place, seed, adjoint_work, send_backward)
    grads = spread(back_outputs, 0)
    stem_back = lax.dot_general(
        grads.reshape(-1, CH),
        stem_weight,
        (((1,), (1,)), ((), ())),
        preferred_element_type=jnp.float32,
    )
    stem_back = stem_back.reshape(number, GRID * GRID, columns_here)
    pixel_grad = (weighted + root_level * stem_back).reshape(
        number, GRID * GRID, columns_here // 3, 3
    )
    hue_part = jnp.sum(pixel_grad * apply_map(hue_slope, pixels), axis=(1, 2, 3))
    sat_part = jnp.sum(pixel_grad * apply_map(sat_slope, pixels), axis=(1, 2, 3))
    colour_grad = section_total(jnp.stack([hue_part, sat_part], axis=1))
    return (purified, colour_grad)


def solution(mesh):
    in_specs = (
        P("batch", None, "section"),
        P("batch", None, "section"),
        P("batch", None, "section"),
        P("batch"),
        P("batch"),
        P("batch"),
        P("section", None),
        P("section", "batch", None),
        P("section", None, None),
        P(None, "section"),
    )
    out_specs = (P("batch", None, "section"), P("batch", None))
    return jax.shard_map(local, mesh=mesh, in_specs=in_specs, out_specs=out_specs, check_vma=False)
```

profile of v0, /device:TPU:0, one launch (start us, length us, event | category | flops | bytes accessed | tf_op | source)
XLA Modules:
  0.0 400.9 jit_solution(12375936215744181771)
XLA Ops:
  8.9 3.1 copy.20
  12.0 3.4 copy.21
  15.4 3.4 multiply_reduce_fusion.2
  18.9 3.3 copy.22
  22.2 3.4 copy.23
  28.1 3.2 convolution_convert_fusion.2
  34.0 3.4 fusion.58
  37.4 27.4 %all-reduce.18.cloned.1.call-done = (bf16[2,64,1024]{2,1,0:T(8,128)(2,1)}, bf16[2,64,1024]{2,1,0:T(8,128)(2,1)}) async-done(((bf16[2,64,1024]{2,1,0:T(8,128)(2,1)}, bf16[2,64,1024]{2,1,0:T(8,128)(2,1)}), (bf16[2,64,1024]{2,1,0:T(8,128)(2,1)}, bf16[2,64,1024]{2,1,0:T(8,128)(2,1)})) %all-reduce.18.cloned.1.call-update) | async-done | bytes 524304 | tf_op jit(solution)/shard_map/psum | solution.py:101
  64.8 72.1 %all-gather.2.cloned.1.call-done = bf16[1,9216,1024]{2,1,0:T(8,128)(2,1)} async-done(((bf16[1,576,1024]{2,1,0:T(8,128)(2,1)}), bf16[1,9216,1024]{2,1,0:T(8,128)(2,1)}) %all-gather.2.cloned.1.call-update) | async-done | bytes 18874384 | tf_op jit(solution)/shard_map/all_gather | solution.py:165
  138.3 72.6 %while.34 = (s32[]{:T(128)}, bf16[64,1024]{1,0:T(8,128)(2,1)}, bf16[2,64,1024]{2,1,0:T(8,128)(2,1)S(1)}, bf16[2,64,1024]{2,1,0:T(8,128)(2,1)}, s32[]{:T(128)}, /...) while((s32[]{:T(128)}, bf16[64,1024]{1,0:T(8,128)(2,1)}, ...), condition=%wide.region_12.13_spmd, body=%wide.region_5.12_spmd.sunk | while | flops 1210057728 | bytes 25409360 | solution.py:145
  139.3 18.3 %conditional.4 = (bf16[64,1024]{1,0:T(8,128)(2,1)S(1)}) conditional(s32[]{:T(128)} %convert_element_type.245, bf16[64,1024]{1,0:T(8,128)(2,1)S(1)} %get-tuple-element.587, (bf16[64,1024]{1,0:T(8,128)(2,1)S(1)}, s32[]{:T(128)}, f32[2,2048]{1,0:T(2,128)}, bf16[9216,1024]{1,0:T(8,128)(2,1)}) %tuple.116), branch_computations={%region_6.6_spmd, %region_7.11_spmd} | conditional | flops 1209861120 | bytes 23311430 | solution.py:139
  147.8 9.8 %fusion = bf16[64,1024]{1,0:T(8,128)(2,1)S(1)} fusion(bf16[64,9216]{1,0:T(8,128)(2,1)S(1)} %fusion.32, bf16[9216,1024]{1,0:T(8,128)(2,1)} %get-tuple-element.369, bf16[64,1024]{1,0:T(8,128)(2,1)S(1)} %get-tuple-element.366), kind=kOutput, calls=%fused_computation.1 | convolution fusion | flops 1208156160 | bytes 20316160 | tf_op jit(solution)/shard_map/while/body/eval_jaxpr/cond/branch_1_fun/dot_general | solution.py:80
  159.3 4.1 %collective-permute-done = bf16[64,1024]{1,0:T(8,128)(2,1)} collective-permute-done((bf16[64,1024]{1,0:T(8,128)(2,1)S(1)}, bf16[64,1024]{1,0:T(8,128)(2,1)}, u32[]{:S(2)}, u32[]{:S(2)}) %collective-permute-start) | collective-permute-done | bytes 131104 | tf_op jit(solution)/shard_map/while/body/eval_jaxpr/ppermute | solution.py:18
  164.5 18.3 %conditional.4 = (bf16[64,1024]{1,0:T(8,128)(2,1)S(1)}) conditional(s32[]{:T(128)} %convert_element_type.245, bf16[64,1024]{1,0:T(8,128)(2,1)S(1)} %get-tuple-element.587, (bf16[64,1024]{1,0:T(8,128)(2,1)S(1)}, s32[]{:T(128)}, f32[2,2048]{1,0:T(2,128)}, bf16[9216,1024]{1,0:T(8,128)(2,1)}) %tuple.116), branch_computations={%region_6.6_spmd, %region_7.11_spmd} | conditional | flops 1209861120 | bytes 23311430 | solution.py:139
  172.9 9.8 %fusion = bf16[64,1024]{1,0:T(8,128)(2,1)S(1)} fusion(bf16[64,9216]{1,0:T(8,128)(2,1)S(1)} %fusion.32, bf16[9216,1024]{1,0:T(8,128)(2,1)} %get-tuple-element.369, bf16[64,1024]{1,0:T(8,128)(2,1)S(1)} %get-tuple-element.366), kind=kOutput, calls=%fused_computation.1 | convolution fusion | flops 1208156160 | bytes 20316160 | tf_op jit(solution)/shard_map/while/body/eval_jaxpr/cond/branch_1_fun/dot_general | solution.py:80
  184.8 3.1 collective-permute-done
  188.9 19.0 %collective-permute-start = (bf16[64,1024]{1,0:T(8,128)(2,1)S(1)}, bf16[64,1024]{1,0:T(8,128)(2,1)}, u32[]{:S(2)}, u32[]{:S(2)}) collective-permute-start(bf16[64,1024]{1,0:T(8,128)(2,1)S(1)} %get-tuple-element.674), channel_id=1, source_target_pairs={{0,16},{16,0},{1,17},{17,1},{2,18},{18,2},{3,19},{19,3},{4,20},{20... | collective-permute-start | bytes 393224 | tf_op jit(solution)/shard_map/while/body/eval_jaxpr/ppermute | solution.py:18
  212.3 138.6 %while.35 = (s32[]{:T(128)}, bf16[64,1024]{1,0:T(8,128)(2,1)}, bf16[2,64,1024]{2,1,0:T(8,128)(2,1)}, s32[]{:T(128)}, pred[]{:T(512)}, /*index=5*/bf16[2,64,1024]...) while((s32[]{:T(128)}, bf16[64,1024]{1,0:T(8,128)(2,1)}, ...), condition=%wide.region_28.29_spmd, body=%wide.region_15.28_spmd.sunk | while | flops 1212769664 | bytes 27270924 | solution.py:145
  213.3 42.1 %collective-permute-start.1 = (bf16[64,1024]{1,0:T(8,128)(2,1)S(1)}, bf16[64,1024]{1,0:T(8,128)(2,1)}, u32[]{:S(2)}, u32[]{:S(2)}) collective-permute-start(bf16[64,1024]{1,0:T(8,128)(2,1)S(1)} %get-tuple-element.675), channel_id=1, source_target_pairs={{0,16},{16,0},{1,17},{17,1},{2,18},{18,2},{3,19},{19,3},{4,20},{20... | collective-permute-start | bytes 393224 | tf_op jit(solution)/shard_map/while/body/eval_jaxpr/ppermute | solution.py:18
  259.5 40.1 %conditional.5 = (bf16[64,1024]{1,0:T(8,128)(2,1)S(1)}) conditional(s32[]{:T(128)} %convert_element_type.246, bf16[64,1024]{1,0:T(8,128)(2,1)S(1)} %bitcast_select_fusion.7, (bf16[64,1024]{1,0:T(8,128)(2,1)S(1)}, bf16[9216,1024]{1,0:T(8,128)(2,1)}, s32[]{:T(128)}, bf16[2,64,1024]{2,1,0:T(8,128)(2,1)S(1)}, f32[2,2048]{1,0:T(2,128)}) %tuple.118), branch_computations={%region_16.16_spmd, %region_17.27_spmd} | conditional | flops 1212638592 | bytes 25697282 | solution.py:139
  267.2 13.2 %fusion.33 = bf16[1,8,8,9216]{3,2,1,0:T(8,128)(2,1)} fusion(bf16[64,1024]{1,0:T(8,128)(2,1)S(1)} %get-tuple-element.380, bf16[9216,1024]{1,0:T(8,128)(2,1)} %get-tuple-element.381), kind=kOutput, calls=%fused_computation.57 | convolution fusion | flops 1208549376 | bytes 20185088 | tf_op jit(solution)/shard_map/while/body/eval_jaxpr/cond/branch_1_fun/transpose(jvp())/dot_general | solution.py:80
  284.3 3.0 multiply_reduce_fusion
  305.7 40.1 %conditional.5 = (bf16[64,1024]{1,0:T(8,128)(2,1)S(1)}) conditional(s32[]{:T(128)} %convert_element_type.246, bf16[64,1024]{1,0:T(8,128)(2,1)S(1)} %bitcast_select_fusion.7, (bf16[64,1024]{1,0:T(8,128)(2,1)S(1)}, bf16[9216,1024]{1,0:T(8,128)(2,1)}, s32[]{:T(128)}, bf16[2,64,1024]{2,1,0:T(8,128)(2,1)S(1)}, f32[2,2048]{1,0:T(2,128)}) %tuple.118), branch_computations={%region_16.16_spmd, %region_17.27_spmd} | conditional | flops 1212638592 | bytes 25697282 | solution.py:139
  313.4 13.2 %fusion.33 = bf16[1,8,8,9216]{3,2,1,0:T(8,128)(2,1)} fusion(bf16[64,1024]{1,0:T(8,128)(2,1)S(1)} %get-tuple-element.380, bf16[9216,1024]{1,0:T(8,128)(2,1)} %get-tuple-element.381), kind=kOutput, calls=%fused_computation.57 | convolution fusion | flops 1208549376 | bytes 20185088 | tf_op jit(solution)/shard_map/while/body/eval_jaxpr/cond/branch_1_fun/transpose(jvp())/dot_general | solution.py:80
  347.5 3.4 collective-permute-done.1
  353.3 3.3 copy.24
  356.6 3.4 copy.25
  360.0 3.3 copy.26
  363.3 3.4 copy.27
  366.7 14.6 %all-reduce.16.cloned.1.call-done = (bf16[2,64,1024]{2,1,0:T(8,128)(2,1)}, bf16[2,64,1024]{2,1,0:T(8,128)(2,1)}) async-done(((bf16[2,64,1024]{2,1,0:T(8,128)(2,1)}, bf16[2,64,1024]{2,1,0:T(8,128)(2,1)}), (bf16[2,64,1024]{2,1,0:T(8,128)(2,1)}, bf16[2,64,1024]{2,1,0:T(8,128)(2,1)})) %all-reduce.16.cloned.1.call-update) | async-done | bytes 524304 | tf_op jit(solution)/shard_map/psum | solution.py:23
  381.4 3.8 multiply_reduce_fusion.5
  385.2 4.9 %psum.39 = bf16[2,2]{0,1:T(2,128)(2,1)S(1)} all-reduce(bf16[2,2]{0,1:T(2,128)(2,1)S(1)} %pad_maximum_fusion.1), channel_id=1, replica_groups=mesh['section'=2,'batch'=16] {'section'}, use_global_device_ids=true, to_apply=%region_34.35 | all-reduce | flops 4 | bytes 16 | tf_op jit(solution)/shard_map/psum | solution.py:101
  (189 shorter events, 104.7 us)
Async XLA Ops:
  8.0 23.3 %copy-start = (bf16[1024,1536]{1,0:T(8,128)(2,1)S(1)}, bf16[1024,1536]{1,0:T(8,128)(2,1)}, u32[]{:S(2)}) copy-start(bf16[1024,1536]{1,0:T(8,128)(2,1)} %param.28) | copy-start | bytes 9437188
  8.0 56.8 %all-reduce.18.cloned.1.call-start = ((), (), s32[]{:S(2)}) async-start(), calls=%async_computation.2 | async-start | bytes 1048576 | tf_op jit(solution)/shard_map/psum | solution.py:101
  12.0 3.4 copy-start.6
  12.0 3.4 copy-start.7
  22.2 4.0 %copy-start.8 = (s32[2]{0:T(128)S(1)}, s32[2]{0:T(128)}, u32[]{:S(2)}) copy-start(s32[2]{0:T(128)} %param.24) | copy-start | bytes 28
  26.4 4.8 %copy-start.2 = (f32[2]{0:T(128)}, f32[2]{0:T(128)S(1)}, u32[]{:S(2)}) copy-start(f32[2]{0:T(128)S(1)} %get-tuple-element.477) | copy-start | bytes 28
  26.4 4.8 %copy-start.4 = (f32[2]{0:T(128)}, f32[2]{0:T(128)S(1)}, u32[]{:S(2)}) copy-start(f32[2]{0:T(128)S(1)} %get-tuple-element.479) | copy-start | bytes 28
  33.1 103.8 %all-gather.2.cloned.1.call-start = ((), (), s32[]{:S(2)}) async-start(), calls=%async_computation | async-start | bytes 20054016 | tf_op jit(solution)/shard_map/all_gather | solution.py:165
  33.7 347.6 %all-reduce.16.cloned.1.call-start = ((), (), s32[]{:S(2)}) async-start(), calls=%async_computation.1 | async-start | bytes 1048576 | tf_op jit(solution)/shard_map/psum | solution.py:23
  157.6 5.8 %collective-permute-start = (bf16[64,1024]{1,0:T(8,128)(2,1)S(1)}, bf16[64,1024]{1,0:T(8,128)(2,1)}, u32[]{:S(2)}, u32[]{:S(2)}) collective-permute-start(bf16[64,1024]{1,0:T(8,128)(2,1)S(1)} %get-tuple-element.674), channel_id=1, source_target_pairs={{0,16},{16,0},{1,17},{17,1},{2,18},{18,2},{3,19},{19,3},{4,20},{20... | collective-permute-start | bytes 393224 | tf_op jit(solution)/shard_map/while/body/eval_jaxpr/ppermute | solution.py:18
  182.8 5.1 %collective-permute-start = (bf16[64,1024]{1,0:T(8,128)(2,1)S(1)}, bf16[64,1024]{1,0:T(8,128)(2,1)}, u32[]{:S(2)}, u32[]{:S(2)}) collective-permute-start(bf16[64,1024]{1,0:T(8,128)(2,1)S(1)} %get-tuple-element.674), channel_id=1, source_target_pairs={{0,16},{16,0},{1,17},{17,1},{2,18},{18,2},{3,19},{19,3},{4,20},{20... | collective-permute-start | bytes 393224 | tf_op jit(solution)/shard_map/while/body/eval_jaxpr/ppermute | solution.py:18
  188.9 22.0 %collective-permute-start = (bf16[64,1024]{1,0:T(8,128)(2,1)S(1)}, bf16[64,1024]{1,0:T(8,128)(2,1)}, u32[]{:S(2)}, u32[]{:S(2)}) collective-permute-start(bf16[64,1024]{1,0:T(8,128)(2,1)S(1)} %get-tuple-element.674), channel_id=1, source_target_pairs={{0,16},{16,0},{1,17},{17,1},{2,18},{18,2},{3,19},{19,3},{4,20},{20... | collective-permute-start | bytes 393224 | tf_op jit(solution)/shard_map/while/body/eval_jaxpr/ppermute | solution.py:18
  213.3 45.2 %collective-permute-start.1 = (bf16[64,1024]{1,0:T(8,128)(2,1)S(1)}, bf16[64,1024]{1,0:T(8,128)(2,1)}, u32[]{:S(2)}, u32[]{:S(2)}) collective-permute-start(bf16[64,1024]{1,0:T(8,128)(2,1)S(1)} %get-tuple-element.675), channel_id=1, source_target_pairs={{0,16},{16,0},{1,17},{17,1},{2,18},{18,2},{3,19},{19,3},{4,20},{20... | collective-permute-start | bytes 393224 | tf_op jit(solution)/shard_map/while/body/eval_jaxpr/ppermute | solution.py:18
  265.2 0.5 copy-start.1
  299.6 5.1 %collective-permute-start.1 = (bf16[64,1024]{1,0:T(8,128)(2,1)S(1)}, bf16[64,1024]{1,0:T(8,128)(2,1)}, u32[]{:S(2)}, u32[]{:S(2)}) collective-permute-start(bf16[64,1024]{1,0:T(8,128)(2,1)S(1)} %get-tuple-element.675), channel_id=1, source_target_pairs={{0,16},{16,0},{1,17},{17,1},{2,18},{18,2},{3,19},{19,3},{4,20},{20... | collective-permute-start | bytes 393224 | tf_op jit(solution)/shard_map/while/body/eval_jaxpr/ppermute | solution.py:18
  311.4 0.5 copy-start.1
  345.8 5.1 %collective-permute-start.1 = (bf16[64,1024]{1,0:T(8,128)(2,1)S(1)}, bf16[64,1024]{1,0:T(8,128)(2,1)}, u32[]{:S(2)}, u32[]{:S(2)}) collective-permute-start(bf16[64,1024]{1,0:T(8,128)(2,1)S(1)} %get-tuple-element.675), channel_id=1, source_target_pairs={{0,16},{16,0},{1,17},{17,1},{2,18},{18,2},{3,19},{19,3},{4,20},{20... | collective-permute-start | bytes 393224 | tf_op jit(solution)/shard_map/while/body/eval_jaxpr/ppermute | solution.py:18
  363.3 18.0 %copy-start.3 = (f32[2]{0:T(128)S(1)}, f32[2]{0:T(128)}, u32[]{:S(2)}) copy-start(f32[2]{0:T(128)} %copy-done.2) | copy-start | bytes 28
  381.4 9.4 %copy-start.5 = (f32[2]{0:T(128)S(1)}, f32[2]{0:T(128)}, u32[]{:S(2)}) copy-start(f32[2]{0:T(128)} %copy-done.4) | copy-start | bytes 28
Sparse Core Ops, SparseCore 0:
  33.3 31.5 all-reduce.17
  353.5 27.8 all-reduce.15
Sparse Core Ops, SparseCore 1:
  35.3 101.6 all-gather.1
where the time goes:
time: 404 us; the launch traced here: 401 us
  waiting for transfers between devices  130 us (32%)
  local copies, waits for them, and re-layouts  72.5 us (18%)
  starting transfers between devices  63.8 us (16%)
  matrix products  61.1 us (15%)
  other arithmetic  52.8 us (13%)
  between operations  15.6 us (4%)
  blocking collectives  4.94 us (1%)
    all_gather x1, waiting for transfers between devices, local(): full_conv = lax.all_gather(conv_weight, 'batch', axis=1, tiled=True)[0]  72.1 us
    ppermute x6, starting transfers between devices, shifted(): return lax.ppermute(value, axis, pairs)  63.6 us
    dot_general x4, matrix products, conv_branch(): product = jnp.dot(columns, weight, preferred_element_type=jnp.float32)  46.1 us
    psum x1, waiting for transfers between devices, section_total(): lax.psum(partial_sum.astype(jnp.bfloat16), 'section').astype(jnp.float32)  27.4 us
    reduce_sum x5, local copies, waits for them, and re-layouts, apply_map(): jnp.sum(matrix[:, None, None, :, :] * pixels[:, :, :, None, :], axis=-1)  16.7 us
    ppermute x6, waiting for transfers between devices, shifted(): return lax.ppermute(value, axis, pairs)  15.1 us
    psum x1, waiting for transfers between devices, from_root(): return lax.psum(block, axis)  14.6 us
    reduce_sum x8, other arithmetic, conv_branch(): grouped - centre  11.6 us
  transfers between devices with their start and end apart: 9, of which 9 were waited for; matrix products, arithmetic and copies ran while one was open for 7% of the time, Pallas kernels for 0%

commit v1 on v0

--- a/solution.py
+++ b/solution.py
@@ -12,6 +12,12 @@
 PV = 3072
 
 
+def gather_and_add(value, axis):
+    parts = lax.all_gather(value, axis, axis=0, tiled=False)
+    summed = parts.sum(axis=0)
+    return summed
+
+
 def shifted(value, axis, steps):
     count = lax.axis_size(axis)
     pairs = [(source, (source + steps) % count) for source in range(count)]
@@ -20,7 +26,7 @@
 
 def from_root(block, axis, holder):
     block = jnp.where(lax.axis_index(axis) == holder, block, jnp.zeros_like(block))
-    return lax.psum(block, axis)
+    return gather_and_add(block, axis)
 
 
 def noise_levels(timestep):

time: 404 us -> 393 us (0.973)
  waiting for transfers between devices: 130 us -> 103 us
  blocking collectives: 4.94 us -> 19.3 us
    psum x1 -> x0, waiting for transfers between devices: 14.6 us -> none  [from_root(): return lax.psum(block, axis)]
    all_gather x0 -> x2, blocking collectives: none -> 14.3 us  [gather_and_add(): parts = lax.all_gather(value, axis, axis=0, tiled=False)]
    psum x1, waiting for transfers between devices: 27.4 us -> 13.9 us  [section_total(): lax.psum(partial_sum.astype(jnp.bfloat16), 'section').astype(jnp.float32)]
  transfers between devices with their start and end apart: 9 -> 8, of which waited for: 9 -> 8; matrix products, arithmetic and copies ran while one was open for 7% -> 7% of each run, Pallas kernels for 0% -> 0%
where the time goes in v1:
time: 393 us; the launch traced here: 390 us
  waiting for transfers between devices  103 us (26%)
  local copies, waits for them, and re-layouts  72.7 us (18%)
  starting transfers between devices  64 us (16%)
  matrix products  61.1 us (16%)
  other arithmetic  54.7 us (14%)
  blocking collectives  19.3 us (5%)
  between operations  15.6 us (4%)
    all_gather x1, waiting for transfers between devices, local(): full_conv = lax.all_gather(conv_weight, 'batch', axis=1, tiled=True)[0]  72.1 us
    ppermute x6, starting transfers between devices, shifted(): return lax.ppermute(value, axis, pairs)  63.7 us
    dot_general x4, matrix products, conv_branch(): product = jnp.dot(columns, weight, preferred_element_type=jnp.float32)  46.1 us
    reduce_sum x5, local copies, waits for them, and re-layouts, apply_map(): jnp.sum(matrix[:, None, None, :, :] * pixels[:, :, :, None, :], axis=-1)  16.8 us
    ppermute x6, waiting for transfers between devices, shifted(): return lax.ppermute(value, axis, pairs)  16.2 us
    all_gather x2, blocking collectives, gather_and_add(): parts = lax.all_gather(value, axis, axis=0, tiled=False)  14.3 us
    psum x1, waiting for transfers between devices, section_total(): lax.psum(partial_sum.astype(jnp.bfloat16), 'section').astype(jnp.float32)  13.9 us
    reduce_sum x8, other arithmetic, conv_branch(): grouped - centre  11.7 us
  transfers between devices with their start and end apart: 8, of which 8 were waited for; matrix products, arithmetic and copies ran while one was open for 7% of the time, Pallas kernels for 0%

profile of v1, /device:TPU:0, one launch (start us, length us, event | category | flops | bytes accessed | tf_op | source)
XLA Modules:
  0.0 390.3 jit_solution(10560083627125310833)
XLA Ops:
  8.9 3.1 copy.26
  12.0 3.4 copy.27
  15.4 3.5 multiply_reduce_fusion.2
  18.9 3.3 copy.28
  22.2 3.4 copy.29
  28.2 3.2 convolution_convert_fusion.2
  33.8 3.3 copy.30
  37.2 3.4 copy.31
  40.5 3.3 copy.32
  43.9 3.5 copy.33
  47.5 3.5 fusion.58
  51.0 13.9 %all-reduce.14.cloned.1.call-done = (bf16[2,64,1024]{2,1,0:T(8,128)(2,1)}, bf16[2,64,1024]{2,1,0:T(8,128)(2,1)}) async-done(((bf16[2,64,1024]{2,1,0:T(8,128)(2,1)}, bf16[2,64,1024]{2,1,0:T(8,128)(2,1)}), (bf16[2,64,1024]{2,1,0:T(8,128)(2,1)}, bf16[2,64,1024]{2,1,0:T(8,128)(2,1)})) %all-reduce.14.cloned.1.call-update) | async-done | bytes 524304 | tf_op jit(solution)/shard_map/psum | solution.py:107
  64.9 72.1 %all-gather.4.cloned.1.call-done = bf16[1,9216,1024]{2,1,0:T(8,128)(2,1)} async-done(((bf16[1,576,1024]{2,1,0:T(8,128)(2,1)}), bf16[1,9216,1024]{2,1,0:T(8,128)(2,1)}) %all-gather.4.cloned.1.call-update) | async-done | bytes 18874384 | tf_op jit(solution)/shard_map/all_gather | solution.py:171
  138.4 72.6 %while.34 = (s32[]{:T(128)}, bf16[64,1024]{1,0:T(8,128)(2,1)}, bf16[2,64,1024]{2,1,0:T(8,128)(2,1)S(1)}, bf16[2,64,1024]{2,1,0:T(8,128)(2,1)}, s32[]{:T(128)}, /...) while((s32[]{:T(128)}, bf16[64,1024]{1,0:T(8,128)(2,1)}, ...), condition=%wide.region_12.13_spmd, body=%wide.region_5.12_spmd.sunk | while | flops 1210057728 | bytes 25409360 | solution.py:151
  139.4 18.3 %conditional.4 = (bf16[64,1024]{1,0:T(8,128)(2,1)S(1)}) conditional(s32[]{:T(128)} %convert_element_type.249, bf16[64,1024]{1,0:T(8,128)(2,1)S(1)} %get-tuple-element.587, (bf16[64,1024]{1,0:T(8,128)(2,1)S(1)}, s32[]{:T(128)}, f32[2,2048]{1,0:T(2,128)}, bf16[9216,1024]{1,0:T(8,128)(2,1)}) %tuple.117), branch_computations={%region_6.6_spmd, %region_7.11_spmd} | conditional | flops 1209861120 | bytes 23311430 | solution.py:145
  147.9 9.8 %fusion = bf16[64,1024]{1,0:T(8,128)(2,1)S(1)} fusion(bf16[64,9216]{1,0:T(8,128)(2,1)S(1)} %fusion.32, bf16[9216,1024]{1,0:T(8,128)(2,1)} %get-tuple-element.369, bf16[64,1024]{1,0:T(8,128)(2,1)S(1)} %get-tuple-element.366), kind=kOutput, calls=%fused_computation.1 | convolution fusion | flops 1208156160 | bytes 20316160 | tf_op jit(solution)/shard_map/while/body/eval_jaxpr/cond/branch_1_fun/dot_general | solution.py:86
  159.4 4.1 %collective-permute-done = bf16[64,1024]{1,0:T(8,128)(2,1)} collective-permute-done((bf16[64,1024]{1,0:T(8,128)(2,1)S(1)}, bf16[64,1024]{1,0:T(8,128)(2,1)}, u32[]{:S(2)}, u32[]{:S(2)}) %collective-permute-start) | collective-permute-done | bytes 131104 | tf_op jit(solution)/shard_map/while/body/eval_jaxpr/ppermute | solution.py:24
  164.6 18.3 %conditional.4 = (bf16[64,1024]{1,0:T(8,128)(2,1)S(1)}) conditional(s32[]{:T(128)} %convert_element_type.249, bf16[64,1024]{1,0:T(8,128)(2,1)S(1)} %get-tuple-element.587, (bf16[64,1024]{1,0:T(8,128)(2,1)S(1)}, s32[]{:T(128)}, f32[2,2048]{1,0:T(2,128)}, bf16[9216,1024]{1,0:T(8,128)(2,1)}) %tuple.117), branch_computations={%region_6.6_spmd, %region_7.11_spmd} | conditional | flops 1209861120 | bytes 23311430 | solution.py:145
  173.0 9.8 %fusion = bf16[64,1024]{1,0:T(8,128)(2,1)S(1)} fusion(bf16[64,9216]{1,0:T(8,128)(2,1)S(1)} %fusion.32, bf16[9216,1024]{1,0:T(8,128)(2,1)} %get-tuple-element.369, bf16[64,1024]{1,0:T(8,128)(2,1)S(1)} %get-tuple-element.366), kind=kOutput, calls=%fused_computation.1 | convolution fusion | flops 1208156160 | bytes 20316160 | tf_op jit(solution)/shard_map/while/body/eval_jaxpr/cond/branch_1_fun/dot_general | solution.py:86
  184.9 3.1 collective-permute-done
  189.0 19.0 %collective-permute-start = (bf16[64,1024]{1,0:T(8,128)(2,1)S(1)}, bf16[64,1024]{1,0:T(8,128)(2,1)}, u32[]{:S(2)}, u32[]{:S(2)}) collective-permute-start(bf16[64,1024]{1,0:T(8,128)(2,1)S(1)} %get-tuple-element.672), channel_id=1, source_target_pairs={{0,16},{16,0},{1,17},{17,1},{2,18},{18,2},{3,19},{19,3},{4,20},{20... | collective-permute-start | bytes 393224 | tf_op jit(solution)/shard_map/while/body/eval_jaxpr/ppermute | solution.py:24
  212.4 140.0 %while.35 = (s32[]{:T(128)}, bf16[64,1024]{1,0:T(8,128)(2,1)}, bf16[2,64,1024]{2,1,0:T(8,128)(2,1)}, s32[]{:T(128)}, pred[]{:T(512)}, /*index=5*/bf16[2,64,1024]...) while((s32[]{:T(128)}, bf16[64,1024]{1,0:T(8,128)(2,1)}, ...), condition=%wide.region_28.29_spmd, body=%wide.region_15.28_spmd.sunk | while | flops 1212769664 | bytes 27270924 | solution.py:151
  213.4 42.2 %collective-permute-start.1 = (bf16[64,1024]{1,0:T(8,128)(2,1)S(1)}, bf16[64,1024]{1,0:T(8,128)(2,1)}, u32[]{:S(2)}, u32[]{:S(2)}) collective-permute-start(bf16[64,1024]{1,0:T(8,128)(2,1)S(1)} %get-tuple-element.673), channel_id=1, source_target_pairs={{0,16},{16,0},{1,17},{17,1},{2,18},{18,2},{3,19},{19,3},{4,20},{20... | collective-permute-start | bytes 393224 | tf_op jit(solution)/shard_map/while/body/eval_jaxpr/ppermute | solution.py:24
  259.7 40.2 %conditional.5 = (bf16[64,1024]{1,0:T(8,128)(2,1)S(1)}) conditional(s32[]{:T(128)} %convert_element_type.250, bf16[64,1024]{1,0:T(8,128)(2,1)S(1)} %bitcast_select_fusion.7, (bf16[64,1024]{1,0:T(8,128)(2,1)S(1)}, bf16[9216,1024]{1,0:T(8,128)(2,1)}, s32[]{:T(128)}, bf16[2,64,1024]{2,1,0:T(8,128)(2,1)S(1)}, f32[2,2048]{1,0:T(2,128)}) %tuple.119), branch_computations={%region_16.16_spmd, %region_17.27_spmd} | conditional | flops 1212638592 | bytes 25697282 | solution.py:145
  267.4 13.2 %fusion.33 = bf16[1,8,8,9216]{3,2,1,0:T(8,128)(2,1)} fusion(bf16[64,1024]{1,0:T(8,128)(2,1)S(1)} %get-tuple-element.380, bf16[9216,1024]{1,0:T(8,128)(2,1)} %get-tuple-element.381), kind=kOutput, calls=%fused_computation.57 | convolution fusion | flops 1208549376 | bytes 20185088 | tf_op jit(solution)/shard_map/while/body/eval_jaxpr/cond/branch_1_fun/transpose(jvp())/dot_general | solution.py:86
  306.0 40.2 %conditional.5 = (bf16[64,1024]{1,0:T(8,128)(2,1)S(1)}) conditional(s32[]{:T(128)} %convert_element_type.250, bf16[64,1024]{1,0:T(8,128)(2,1)S(1)} %bitcast_select_fusion.7, (bf16[64,1024]{1,0:T(8,128)(2,1)S(1)}, bf16[9216,1024]{1,0:T(8,128)(2,1)}, s32[]{:T(128)}, bf16[2,64,1024]{2,1,0:T(8,128)(2,1)S(1)}, f32[2,2048]{1,0:T(2,128)}) %tuple.119), branch_computations={%region_16.16_spmd, %region_17.27_spmd} | conditional | flops 1212638592 | bytes 25697282 | solution.py:145
  313.7 13.2 %fusion.33 = bf16[1,8,8,9216]{3,2,1,0:T(8,128)(2,1)} fusion(bf16[64,1024]{1,0:T(8,128)(2,1)S(1)} %get-tuple-element.380, bf16[9216,1024]{1,0:T(8,128)(2,1)} %get-tuple-element.381), kind=kOutput, calls=%fused_computation.57 | convolution fusion | flops 1208549376 | bytes 20185088 | tf_op jit(solution)/shard_map/while/body/eval_jaxpr/cond/branch_1_fun/transpose(jvp())/dot_general | solution.py:86
  347.9 4.5 %collective-permute-done.1 = bf16[64,1024]{1,0:T(8,128)(2,1)} collective-permute-done((bf16[64,1024]{1,0:T(8,128)(2,1)S(1)}, bf16[64,1024]{1,0:T(8,128)(2,1)}, u32[]{:S(2)}, u32[]{:S(2)}) %collective-permute-start.1) | collective-permute-done | bytes 131104 | tf_op jit(solution)/shard_map/while/body/eval_jaxpr/ppermute | solution.py:24
  353.4 7.2 %all-gather.1 = bf16[4,64,1024]{2,1,0:T(8,128)(2,1)} all-gather(bf16[2,64,1024]{2,1,0:T(8,128)(2,1)S(1)} %broadcast_select_fusion), channel_id=3, replica_groups=mesh['section'=2,'batch'=16] {'section'}, dimensions={0}, use_global_device_ids=true | all-gather | bytes 786432 | tf_op jit(solution)/shard_map/all_gather | solution.py:16
  362.4 3.8 multiply_reduce_fusion.5
  366.3 4.9 %psum.23 = bf16[2,2]{0,1:T(2,128)(2,1)S(1)} all-reduce(bf16[2,2]{0,1:T(2,128)(2,1)S(1)} %pad_maximum_fusion.1), channel_id=1, replica_groups=mesh['section'=2,'batch'=16] {'section'}, use_global_device_ids=true, to_apply=%region_34.35 | all-reduce | flops 4 | bytes 16 | tf_op jit(solution)/shard_map/psum | solution.py:107
  372.0 7.2 %all-gather = bf16[4,64,1024]{2,1,0:T(8,128)(2,1)} all-gather(bf16[2,64,1024]{2,1,0:T(8,128)(2,1)S(1)} %broadcast_select_fusion.1), channel_id=2, replica_groups=mesh['section'=2,'batch'=16] {'section'}, dimensions={0}, use_global_device_ids=true | all-gather | bytes 786432 | tf_op jit(solution)/shard_map/all_gather | solution.py:16
  (192 shorter events, 109.4 us)
Async XLA Ops:
  8.0 23.3 %copy-start = (bf16[1024,1536]{1,0:T(8,128)(2,1)S(1)}, bf16[1024,1536]{1,0:T(8,128)(2,1)}, u32[]{:S(2)}) copy-start(bf16[1024,1536]{1,0:T(8,128)(2,1)} %param.28) | copy-start | bytes 9437188
  8.0 56.9 %all-reduce.14.cloned.1.call-start = ((), (), s32[]{:S(2)}) async-start(), calls=%async_computation.1 | async-start | bytes 1048576 | tf_op jit(solution)/shard_map/psum | solution.py:107
  12.0 3.4 copy-start.7
  12.0 3.4 copy-start.8
  22.2 4.1 %copy-start.9 = (s32[2]{0:T(128)S(1)}, s32[2]{0:T(128)}, u32[]{:S(2)}) copy-start(s32[2]{0:T(128)} %param.24) | copy-start | bytes 28
  26.5 4.8 %copy-start.3 = (f32[2]{0:T(128)}, f32[2]{0:T(128)S(1)}, u32[]{:S(2)}) copy-start(f32[2]{0:T(128)S(1)} %get-tuple-element.477) | copy-start | bytes 28
  26.5 4.8 %copy-start.5 = (f32[2]{0:T(128)}, f32[2]{0:T(128)S(1)}, u32[]{:S(2)}) copy-start(f32[2]{0:T(128)S(1)} %get-tuple-element.479) | copy-start | bytes 28
  33.2 103.8 %all-gather.4.cloned.1.call-start = ((), (), s32[]{:S(2)}) async-start(), calls=%async_computation | async-start | bytes 20054016 | tf_op jit(solution)/shard_map/all_gather | solution.py:171
  157.7 5.8 %collective-permute-start = (bf16[64,1024]{1,0:T(8,128)(2,1)S(1)}, bf16[64,1024]{1,0:T(8,128)(2,1)}, u32[]{:S(2)}, u32[]{:S(2)}) collective-permute-start(bf16[64,1024]{1,0:T(8,128)(2,1)S(1)} %get-tuple-element.672), channel_id=1, source_target_pairs={{0,16},{16,0},{1,17},{17,1},{2,18},{18,2},{3,19},{19,3},{4,20},{20... | collective-permute-start | bytes 393224 | tf_op jit(solution)/shard_map/while/body/eval_jaxpr/ppermute | solution.py:24
  182.9 5.1 %collective-permute-start = (bf16[64,1024]{1,0:T(8,128)(2,1)S(1)}, bf16[64,1024]{1,0:T(8,128)(2,1)}, u32[]{:S(2)}, u32[]{:S(2)}) collective-permute-start(bf16[64,1024]{1,0:T(8,128)(2,1)S(1)} %get-tuple-element.672), channel_id=1, source_target_pairs={{0,16},{16,0},{1,17},{17,1},{2,18},{18,2},{3,19},{19,3},{4,20},{20... | collective-permute-start | bytes 393224 | tf_op jit(solution)/shard_map/while/body/eval_jaxpr/ppermute | solution.py:24
  189.0 22.0 %collective-permute-start = (bf16[64,1024]{1,0:T(8,128)(2,1)S(1)}, bf16[64,1024]{1,0:T(8,128)(2,1)}, u32[]{:S(2)}, u32[]{:S(2)}) collective-permute-start(bf16[64,1024]{1,0:T(8,128)(2,1)S(1)} %get-tuple-element.672), channel_id=1, source_target_pairs={{0,16},{16,0},{1,17},{17,1},{2,18},{18,2},{3,19},{19,3},{4,20},{20... | collective-permute-start | bytes 393224 | tf_op jit(solution)/shard_map/while/body/eval_jaxpr/ppermute | solution.py:24
  213.4 45.3 %collective-permute-start.1 = (bf16[64,1024]{1,0:T(8,128)(2,1)S(1)}, bf16[64,1024]{1,0:T(8,128)(2,1)}, u32[]{:S(2)}, u32[]{:S(2)}) collective-permute-start(bf16[64,1024]{1,0:T(8,128)(2,1)S(1)} %get-tuple-element.673), channel_id=1, source_target_pairs={{0,16},{16,0},{1,17},{17,1},{2,18},{18,2},{3,19},{19,3},{4,20},{20... | collective-permute-start | bytes 393224 | tf_op jit(solution)/shard_map/while/body/eval_jaxpr/ppermute | solution.py:24
  265.4 0.5 copy-start.2
  299.9 5.1 %collective-permute-start.1 = (bf16[64,1024]{1,0:T(8,128)(2,1)S(1)}, bf16[64,1024]{1,0:T(8,128)(2,1)}, u32[]{:S(2)}, u32[]{:S(2)}) collective-permute-start(bf16[64,1024]{1,0:T(8,128)(2,1)S(1)} %get-tuple-element.673), channel_id=1, source_target_pairs={{0,16},{16,0},{1,17},{17,1},{2,18},{18,2},{3,19},{19,3},{4,20},{20... | collective-permute-start | bytes 393224 | tf_op jit(solution)/shard_map/while/body/eval_jaxpr/ppermute | solution.py:24
  311.7 0.5 copy-start.2
  346.2 6.2 %collective-permute-start.1 = (bf16[64,1024]{1,0:T(8,128)(2,1)S(1)}, bf16[64,1024]{1,0:T(8,128)(2,1)}, u32[]{:S(2)}, u32[]{:S(2)}) collective-permute-start(bf16[64,1024]{1,0:T(8,128)(2,1)S(1)} %get-tuple-element.673), channel_id=1, source_target_pairs={{0,16},{16,0},{1,17},{17,1},{2,18},{18,2},{3,19},{19,3},{4,20},{20... | collective-permute-start | bytes 393224 | tf_op jit(solution)/shard_map/while/body/eval_jaxpr/ppermute | solution.py:24
  352.4 10.0 %copy-start.4 = (f32[2]{0:T(128)S(1)}, f32[2]{0:T(128)}, u32[]{:S(2)}) copy-start(f32[2]{0:T(128)} %copy-done.3) | copy-start | bytes 28
  362.4 9.5 %copy-start.1 = (bf16[2,64,1024]{2,1,0:T(8,128)(2,1)S(1)}, bf16[2,64,1024]{2,1,0:T(8,128)(2,1)}, u32[]{:S(2)}) copy-start(bf16[2,64,1024]{2,1,0:T(8,128)(2,1)} %get-tuple-element.400) | copy-start | bytes 786436
  366.3 14.0 %copy-start.6 = (f32[2]{0:T(128)S(1)}, f32[2]{0:T(128)}, u32[]{:S(2)}) copy-start(f32[2]{0:T(128)} %copy-done.5) | copy-start | bytes 28
Sparse Core Ops, SparseCore 0:
  33.3 31.5 all-reduce.13
Sparse Core Ops, SparseCore 1:
  35.4 101.6 all-gather.3
